TPU v7x, 256 devices: a whole 4x4x8 slice. The times are simulated.
256 devices in a mesh: rows: 64 (over z, y, core), cols: 4 (over x).
Axes of the slice: x: 4, y: 4, z: 8, core: 2. Of those that a mesh axis runs over, the one named last changes fastest.
Arguments:
- train_points: float32 [8, 4, 16384], replicated, may hold values from -1.2 to 1.2
- length_scales: float32 [8], replicated, may hold values from 0.4 to 1.2
- test_points: float32 [8, 4, 2048], P(None, 'cols', 'rows'), may hold values from -1.2 to 1.2
- lower_panel: float32 [4, 512, 16384], P(None, None, 'rows'), as said below
Outputs:
- solved: float32 [4, 8192, 16384], P(None, 'cols', 'rows')
Inputs may be any that keep to these rules, and one draw needn't show every extreme that they name: L is lower triangular: lower_panel[0, j, position] is zero where j > position, and its diagonal entries lie in 1 to 2.
All inputs are finite; a program needn't handle non-finite values.
Results may differ from a plain program's by a relative error of at most 0.0001.
Values sent between devices are 32-bit elements; how exact they have to be, the bound alone decides.
A program may use at most 64 MiB of HBM per device.

v0:
```python
import jax
import jax.numpy as jnp
from jax import lax
from jax.sharding import PartitionSpec as P


def spread(array, axis, root):
    mine = lax.axis_index(axis) == root
    return lax.psum(jnp.where(mine, array, jnp.zeros_like(array)), axis)


def kernel_block(train_rows, length_scales, tests):
    total = jnp.zeros((tests.shape[1], train_rows.shape[1]), jnp.float32)
    for feature in range(train_rows.shape[0]):
        differ = (tests[feature][:, None] - train_rows[feature][None, :]) / length_scales[feature]
        total = total + differ * differ
    return jnp.exp(-0.5 * total)


def upper_solve(upper, rights):
    order = upper.shape[0]
    eye_rows = lax.broadcasted_iota(jnp.int32, (order, order), 0)
    eye_cols = lax.broadcasted_iota(jnp.int32, (order, order), 1)
    identity = jnp.where(eye_rows == eye_cols, 1.0, 0.0).astype(jnp.float32)
    diag_values = jnp.sum(upper * identity, axis=1)
    strict = jnp.where(eye_cols > eye_rows, upper, 0.0) / diag_values[:, None]
    power = -strict
    inverse = identity + power
    for level in range((order - 1).bit_length() - 1):
        power = jnp.dot(power, power, precision=lax.Precision.HIGHEST)
        inverse = jnp.dot(inverse, identity + power, precision=lax.Precision.HIGHEST)
    inverse = inverse / diag_values[None, :]
    return jnp.dot(rights, inverse, precision=lax.Precision.HIGHEST)


def per_device(train_points, length_scales, test_points, lower_panel):
    block_rows = lower_panel.shape[2]
    steps_count = lower_panel.shape[1] // block_rows
    rounds_count = lower_panel.shape[0]
    my_index = lax.axis_index("rows")
    tests = lax.all_gather(test_points, "rows", axis=2, tiled=True)[:, 0, :]
    mine = lax.dynamic_slice_in_dim(train_points, my_index * block_rows, block_rows, 2)
    kstar = jnp.stack(
        [kernel_block(mine[:, r, :], length_scales, tests) for r in range(rounds_count)], axis=0
    )
    for k in range(steps_count):
        lower = k * block_rows
        own = kstar[0]
        diag = lower_panel[0, lower : lower + block_rows, :]
        solution = jnp.where(my_index == k, upper_solve(diag, own), 0.0)
        slab = spread(solution, "rows", k)
        update = jnp.einsum(
            "cj,rji->rci",
            slab,
            lower_panel[:, lower : lower + block_rows, :],
            precision=lax.Precision.HIGHEST,
        )
        kstar = kstar - update
        first = jnp.where(my_index == k, slab, kstar[0])
        kstar = kstar.at[0].set(first)
    return kstar


def solution(mesh):
    placed = (P(), P(), P(None, "cols", "rows"), P(None, None, "rows"))
    return jax.shard_map(
        per_device, mesh=mesh, in_specs=placed, out_specs=P(None, "cols", "rows"), check_vma=False
    )
```

profile of v0, /device:TPU:37, one launch (start us, length us, event | category | flops | bytes accessed | tf_op | source)
XLA Modules:
  0.0 548.6 jit_solution(13010042762640370917)
XLA Ops:
  6.5 1.2 fusion.75
  7.7 1.5 fusion.87
  9.3 1.4 fusion.69
  10.7 0.4 fusion.160
  11.1 0.7 fusion.159
  11.7 0.1 copy.6
  11.8 53.4 %all_gather.3 = f32[8,1,2048]{0,1,2:T(1,128)S(1)} all-gather(f32[8,1,32]{0,1,2:T(1,128)S(1)} %copy.6), channel_id=1, replica_groups=mesh['rows'=64,'cols'=4] {'rows'}, dimensions={2}, use_global_device_ids=true | all-gather | bytes 66560 | tf_op jit(solution)/shard_map/all_gather | solution.py:41
  65.2 53.1 %slice_reduce_fusion.7 = (f32[2048]{0:T(1024)S(1)}, f32[2048]{0:T(1024)S(1)}, f32[2048]{0:T(1024)S(1)}, f32[2048]{0:T(1024)S(1)}, f32[2048]{0:T(1024)S(1)}, /*in...) fusion(f32[8,1,2048]{0,1,2:T(1,128)S(1)} %all_gather.3), kind=kLoop, calls=%fused_computation.79 | loop fusion | bytes 131072 | tf_op jit(solution)/shard_map/slice | solution.py:15
  118.2 0.4 fusion.161
  118.6 0.4 fusion.70
  119.0 0.4 fusion.162
  119.4 0.4 fusion.71
  119.8 0.4 fusion.163
  120.2 0.4 fusion.72
  120.6 0.4 fusion.164
  121.0 0.4 fusion.73
  121.4 0.4 select_add_fusion.8
  121.8 0.4 fusion.74
  122.2 0.4 convolution_divide_fusion.1
  122.6 1.2 constant_dynamic-slice_fusion.9
  123.8 11.6 %fusion.1 = f32[2048,256]{1,0:T(8,128)} fusion(f32[256,256]{1,0:T(8,128)S(1)} %convolution_divide_fusion.1, f32[]{:T(128)} %bitcast.15, f32[256]{0:T(256)S(1)} %bitcast.161, f32[2048]{0:T(1024)S(1)} %get-tuple-element.32, f32[]{:T(128)} %bitcast.13, f32[256]{0:T(256)S(1)} %bitcast.163, f32[2048]{0:T(1024)S(1)} %get-tuple-element.33, f32[]{:T(128)} %bitcast.11, ...), kind=kOutput, calls=%fused_computation.5 | convolution fusion | flops 1628438528 | bytes 2433057 | tf_op jit(solution)/shard_map/dot_general | solution.py:33
  135.4 7.4 %multiply_exponential_fusion.3 = f32[1,2048,256]{2,1,0:T(8,128)S(1)} fusion(f32[]{:T(128)} %bitcast.15, f32[256]{0:T(256)S(1)} %bitcast.162, f32[2048]{0:T(1024)S(1)} %get-tuple-element.32, f32[]{:T(128)} %bitcast.13, f32[256]{0:T(256)S(1)} %bitcast.164, f32[2048]{0:T(1024)S(1)} %get-tuple-element.33, f32[]{:T(128)} %bitcast.11, f32[256]{0:T(256)S(1)} %bitcast.166, ...), kind=kLoop, calls=%fused_computation.51 | loop fusion | flops 16777216 | bytes 2170912 | tf_op jit(solution)/shard_map/exp | solution.py:17
  142.8 1.5 fusion.82
  144.4 1.4 fusion.76
  145.8 0.4 fusion.165
  146.1 0.4 fusion.166
  146.5 0.4 fusion.77
  146.9 0.4 fusion.167
  147.3 0.4 fusion.78
  147.7 0.4 fusion.168
  148.1 0.4 fusion.79
  148.5 0.4 fusion.169
  148.9 0.4 fusion.80
  149.3 0.4 select_add_fusion
  149.7 0.4 fusion.81
  150.1 0.4 convolution_divide_fusion
  150.5 9.7 %multiply_exponential_fusion = f32[1,2048,256]{2,1,0:T(8,128)} fusion(f32[256]{0:T(256)S(1)} %bitcast.158, f32[256]{0:T(256)S(1)} %bitcast.151, f32[256]{0:T(256)S(1)} %bitcast.152, f32[256]{0:T(256)S(1)} %bitcast.153, f32[256]{0:T(256)S(1)} %bitcast.154, f32[256]{0:T(256)S(1)} %bitcast.155, f32[256]{0:T(256)S(1)} %bitcast.156, f32[256]{0:T(256)S(1)} %bitcast.157, ...), kind=kLoop, calls=%fused_computation.48 | loop fusion | flops 16777216 | bytes 2170912 | tf_op jit(solution)/shard_map/exp | solution.py:17
  160.2 9.7 %multiply_exponential_fusion.1 = f32[1,2048,256]{2,1,0:T(8,128)} fusion(f32[256]{0:T(256)S(1)} %bitcast.143, f32[256]{0:T(256)S(1)} %bitcast.144, f32[256]{0:T(256)S(1)} %bitcast.145, f32[256]{0:T(256)S(1)} %bitcast.146, f32[256]{0:T(256)S(1)} %bitcast.147, f32[256]{0:T(256)S(1)} %bitcast.148, f32[256]{0:T(256)S(1)} %bitcast.149, f32[256]{0:T(256)S(1)} %bitcast.150, ...), kind=kLoop, calls=%fused_computation.49 | loop fusion | flops 16777216 | bytes 2170912 | tf_op jit(solution)/shard_map/exp | solution.py:17
  169.9 9.7 %multiply_exponential_fusion.2 = f32[1,2048,256]{2,1,0:T(8,128)} fusion(f32[256]{0:T(256)S(1)} %bitcast.135, f32[256]{0:T(256)S(1)} %bitcast.136, f32[256]{0:T(256)S(1)} %bitcast.137, f32[256]{0:T(256)S(1)} %bitcast.138, f32[256]{0:T(256)S(1)} %bitcast.139, f32[256]{0:T(256)S(1)} %bitcast.140, f32[256]{0:T(256)S(1)} %bitcast.141, f32[256]{0:T(256)S(1)} %bitcast.142, ...), kind=kLoop, calls=%fused_computation.50 | loop fusion | flops 16777216 | bytes 2170912 | tf_op jit(solution)/shard_map/exp | solution.py:17
  179.6 140.9 %all-reduce.3.cloned.1.call-done = f32[2048,256]{1,0:T(8,128)} async-done(((f32[2048,256]{1,0:T(8,128)}), f32[2048,256]{1,0:T(8,128)}) %all-reduce.3.cloned.1.call-update) | async-done | bytes 2097168 | tf_op jit(solution)/shard_map/psum | solution.py:9
  320.5 10.6 %maximum_subtract_fusion = f32[4,2048,256]{2,1,0:T(8,128)S(1)} fusion(f32[1,2048,256]{2,1,0:T(8,128)} %multiply_exponential_fusion, f32[1,2048,256]{2,1,0:T(8,128)} %multiply_exponential_fusion.1, f32[1,2048,256]{2,1,0:T(8,128)} %multiply_exponential_fusion.2, f32[1,2048,256]{2,1,0:T(8,128)S(1)} %multiply_exponential_fusion.3, ...), kind=kOutput, calls=%fused_computation | convolution fusion | flops 6450839552 | bytes 19922944 | tf_op jit(solution)/shard_map/cj,rji->rci/dot_general | solution.py:52
  331.1 3.4 copy-done
  334.5 0.3 fusion.5
  334.8 3.1 fusion
  337.9 1.5 bitcast_dynamic-update-slice_fusion
  339.4 187.2 %all-reduce.5.cloned.1.call-done = f32[2048,256]{1,0:T(8,128)} async-done(((f32[2048,256]{1,0:T(8,128)}), f32[2048,256]{1,0:T(8,128)}) %all-reduce.5.cloned.1.call-update) | async-done | bytes 2097168 | tf_op jit(solution)/shard_map/psum | solution.py:9
  526.5 12.0 %bitcast_subtract_fusion = f32[4,2048,256]{2,1,0:T(8,128)} fusion(f32[4,2048,256]{2,1,0:T(8,128)} %bitcast_dynamic-update-slice_fusion, f32[2048,256]{1,0:T(8,128)} %all-reduce.5.cloned.1.call-done, f32[4,512,256]{2,1,0:T(8,128)} %param.11), kind=kOutput, calls=%fused_computation.1 | convolution fusion | flops 6444548096 | bytes 19922944 | tf_op jit(solution)/shard_map/cj,rji->rci/dot_general | solution.py:52
  538.5 3.2 fusion.4
  (13 shorter events, 0.1 us)
Async XLA Ops:
  6.5 313.9 %all-reduce.3.cloned.1.call-start = ((), (), s32[]{:S(2)}) async-start(), calls=%async_computation | async-start | bytes 4194304 | tf_op jit(solution)/shard_map/psum | solution.py:9
  6.5 4.5 copy-start.3
  6.5 5.2 copy-start.4
  135.4 391.2 %all-reduce.5.cloned.1.call-start = ((), (), s32[]{:S(2)}) async-start(), calls=%async_computation.1 | async-start | bytes 4194304 | tf_op jit(solution)/shard_map/psum | solution.py:9
  320.5 14.1 %copy-start.1 = (f32[2048,256]{1,0:T(8,128)S(1)}, f32[2048,256]{1,0:T(8,128)}, u32[]{:S(2)}) copy-start(f32[2048,256]{1,0:T(8,128)} %all-reduce.3.cloned.1.call-done) | copy-start | bytes 6291460
  331.1 3.4 copy-start
  526.5 12.0 %copy-start.2 = (f32[2048,256]{1,0:T(8,128)S(1)}, f32[2048,256]{1,0:T(8,128)}, u32[]{:S(2)}) copy-start(f32[2048,256]{1,0:T(8,128)} %all-reduce.5.cloned.1.call-done) | copy-start | bytes 6291460
Sparse Core Ops, SparseCore 0:
  135.5 184.9 all-reduce.2
  338.0 188.4 all-reduce.4
where the time goes:
time: 552 us; the launch traced here: 549 us
  waiting for transfers between devices  328 us (59%)
  local copies, waits for them, and re-layouts  59.8 us (11%)
  blocking collectives  53.4 us (10%)
  matrix products  52.4 us (9%)
  other arithmetic  41.2 us (7%)
  between operations  13.7 us (2%)
    psum x2, waiting for transfers between devices, spread(): return lax.psum(jnp.where(mine, array, jnp.zeros_like(array)), axis)  328 us
    all_gather x1, blocking collectives, per_device(): tests = lax.all_gather(test_points, 'rows', axis=2, tiled=True)[:, 0, :]  53.4 us
    slice x1, local copies, waits for them, and re-layouts, kernel_block(): tests[feature][:, None] - train_rows[feature][None, :]  53.1 us
    exp x4, other arithmetic, kernel_block(): return jnp.exp(-0.5 * total)  36.5 us
    dot_general x2, matrix products, per_device(): jnp.einsum('cj,rji->rci', slab, lower_panel[:, lower:lower + block_rows,...  22.6 us
    dot_general x2, matrix products, upper_solve(): return jnp.dot(rights, inverse, precision=lax.Precision.HIGHEST)  14.7 us
  transfers between devices with their start and end apart: 2, of which 2 were waited for; matrix products, arithmetic and copies ran while one was open for 8% of the time, Pallas kernels for 0%

commit v1 on v0

v1 whole, which is shorter than its diff:
```python
import functools
import math

import jax
import jax.numpy as jnp
from jax import lax
from jax.experimental import pallas as pl
from jax.experimental.pallas import tpu as pltpu
from jax.sharding import PartitionSpec as P

MESH = pl.DeviceIdType.MESH
F32, BF16 = jnp.float32, jnp.bfloat16
LOG2E = math.log2(math.e)

NX, NY, NZ, NC = 4, 4, 8, 2
BLK = 256
HALF = BLK // 2
ROUNDS = 4
DIM = 8
TESTS = 2048
CHUNK = TESTS // NZ
COLS = ROUNDS * BLK
FEAT = 64
PIECE = HALF // NX
TRI = BLK + HALF
SQ = 2 * BLK


def dot(a, b):
    return jnp.dot(a, b, preferred_element_type=F32)


def dot_full(a, b):
    return jnp.dot(a, b, preferred_element_type=F32, precision=lax.Precision.HIGHEST)


def parts3(x):
    h = x.astype(BF16).astype(F32)
    m = (x - h).astype(BF16).astype(F32)
    l = (x - h - m).astype(BF16).astype(F32)
    return h, m, l


def parts2(x):
    h = x.astype(BF16)
    return h, (x - h.astype(F32)).astype(BF16)


def wide(x):
    h, l = parts2(x)
    return jnp.concatenate([h, l, h], axis=1)


def features(points, factor, mirrored):
    n = points.shape[1]
    norm = (-0.5 * LOG2E) * jnp.sum(points * points, axis=0, keepdims=True)
    p1, p2, p3 = parts3(points * factor)
    n1, n2, n3 = parts3(norm)
    row = lax.broadcasted_iota(jnp.int32, (DIM, n), 0)
    base = 3 if mirrored else 0
    own = jnp.where(row == base, n1, jnp.where(row == base + 1, n2, n3))
    mine = (row >= base) & (row < base + 3)
    tail = jnp.where(mine, own, jnp.where(row < 6, 1.0, 0.0))
    order = (p1, p2, p1, p2, p3, p1) if mirrored else (p1, p1, p2, p2, p1, p3)
    return jnp.concatenate(list(order) + [tail, jnp.zeros((DIM, n), F32)], axis=0)


def upper_inverse(u):
    row = lax.broadcasted_iota(jnp.int32, (BLK, BLK), 0)
    col = lax.broadcasted_iota(jnp.int32, (BLK, BLK), 1)
    eye = row == col
    on_diag = jnp.where(eye, u, 0.0)
    d_col = jnp.sum(on_diag, axis=1, keepdims=True)
    d_row = jnp.sum(on_diag, axis=0, keepdims=True)
    strict = jnp.where(col > row, u, 0.0) / d_col
    size = 32
    power = jnp.where(row // size == col // size, -strict, 0.0)
    inverse = jnp.where(eye, 1.0, 0.0) + power
    for _ in range(4):
        power = dot_full(power, power)
        inverse = inverse + dot_full(inverse, power)
    while size < BLK:
        pair = (row // (2 * size) == col // (2 * size)) & (row // size != col // size)
        inverse = inverse - dot_full(dot_full(inverse, jnp.where(pair, strict, 0.0)), inverse)
        size *= 2
    return inverse / d_row


def unpack_tri(packed):
    low = jnp.concatenate([jnp.zeros((HALF, HALF), F32), packed[:, BLK:]], axis=1)
    return jnp.concatenate([packed[:, :BLK], low], axis=0)


def gather_kernel(
    train, scales_hbm, tests_hbm, panel, acc, a0, w0,
    tests, scales, pv, tv, th, tile, slots, group, gathered, feat_t, feat_s, feat_h, a1, w1, p0, p1, p0f,
    vsrc, usrc, gv, gu,
    lsem, sa, ra, sb, rb, sv1, rv1, su1, ru1, sv2, rv2, su2, ru2,
):
    m = lax.axis_index("rows")
    x = lax.axis_index("cols")
    z, y, c = m // 8, (m // 2) % NY, m % 2
    q = m % 8
    is_src = m < 2
    xc = x * 2 + c

    def at(zz, yy, cc, xx):
        return ((zz % NZ) * 8 + (yy % NY) * 2 + cc % 2, xx % NX)

    def in_group(k):
        return (z * 8 + (q + k) % 8, x)

    def in_line(k):
        return at(z + k, y, c, x)

    def in_cross(k):
        o = (xc + k) % 8
        return (z * 8 + y * 2 + o % 2, o // 2)

    loads = [
        pltpu.make_async_copy(panel.at[0], pv.at[0], lsem.at[0]),
        pltpu.make_async_copy(train.at[:, :, pl.ds(pl.multiple_of(m * BLK, BLK), BLK)], tv, lsem.at[1]),
        pltpu.make_async_copy(train.at[:, :, pl.ds(0, 2 * BLK)], th, lsem.at[2]),
        pltpu.make_async_copy(panel.at[pl.ds(1, 3)], pv.at[pl.ds(1, 3)], lsem.at[3]),
        pltpu.make_async_copy(scales_hbm, scales, lsem.at[4]),
    ]
    load_tests = pltpu.make_async_copy(tests_hbm, tests, lsem.at[5])
    load_tests.start()
    for copy in loads:
        copy.start()

    barrier = pltpu.get_barrier_semaphore()
    for k in range(1, 8):
        for who in (in_group(k), in_line(k), in_cross(k)):
            pl.semaphore_signal(barrier, inc=1, device_id=who, device_id_type=MESH)

    @pl.when(jnp.logical_not(is_src))
    def _():
        pl.semaphore_signal(barrier, inc=1, device_id=(c, x), device_id_type=MESH)

    tile[...] = jnp.zeros((DIM, 128), F32)
    load_tests.wait()
    tile[:, pl.ds(0, 32)] = tests[:, 0, :]

    my_rows = pl.ds(pl.multiple_of(x * PIECE, PIECE), PIECE)
    loads[0].wait()

    @pl.when(is_src)
    def _():
        u = pv[0, pl.ds(pl.multiple_of(c * BLK, BLK), BLK), :]
        v = upper_inverse(u)
        vsrc[...] = jnp.concatenate([v[:HALF, :], v[HALF:, HALF:]], axis=1)
        usrc[...] = jnp.concatenate([pv[0, pl.ds(0, HALF), :], pv[0, pl.ds(HALF, HALF), :]], axis=1)

    @pl.when(is_src)
    def _():
        pl.semaphore_wait(barrier, 21 + 31)

    @pl.when(jnp.logical_not(is_src))
    def _():
        pl.semaphore_wait(barrier, 21)

    def remote(src, dst, ssem, rsem, who):
        return pltpu.make_async_remote_copy(
            src_ref=src, dst_ref=dst, send_sem=ssem, recv_sem=rsem, device_id=who, device_id_type=MESH
        )

    def send_a(k):
        return remote(tile, slots.at[q], sa.at[k], ra.at[q], in_group(k))

    def send_b(k):
        return remote(group, gathered.at[z], sb.at[k], rb.at[z], in_line(k))

    def plane(k):
        return at(k // NY, k % NY, c, x)

    def send_v1(k):
        return remote(vsrc.at[my_rows], gv.at[c, my_rows], sv1.at[k], rv1, plane(k))

    def send_u1(k):
        return remote(usrc.at[my_rows], gu.at[my_rows], su1.at[k], ru1, plane(k))

    def send_v2(k):
        return remote(gv.at[c, my_rows], gv.at[c, my_rows], sv2.at[k], rv2.at[c, x], in_cross(k))

    def send_u2(k):
        return remote(gu.at[my_rows], gu.at[my_rows], su2.at[k], ru2.at[x], in_cross(k))

    for k in range(1, 8):
        send_a(k).start()

    @pl.when(is_src & (c == 1))
    def _():
        for k in range(1, 32):
            send_v1(k).start()

    slots[q] = tile[...]
    for k in range(1, 8):
        o = (q + k) % 8
        remote(tile, slots.at[o], sa.at[k], ra.at[o], in_group(k)).wait_recv()
    for h in range(2):
        total = slots[4 * h]
        for j in range(1, 4):
            total = total + pltpu.roll(slots[4 * h + j], 32 * j, 1)
        group[:, pl.ds(128 * h, 128)] = total
    for k in range(1, 8):
        send_b(k).start()
    gathered[z] = group[...]

    @pl.when(is_src & (c == 1))
    def _():
        for k in range(1, 32):
            send_u1(k).start()

    @pl.when(is_src & (c == 0))
    def _():
        for k in range(1, 32):
            send_v1(k).start()

    for copy in loads[1:]:
        copy.wait()
    row8 = lax.broadcasted_iota(jnp.int32, (DIM, 1), 0)
    scale = jnp.zeros((DIM, 1), F32)
    for d in range(DIM):
        scale = jnp.where(row8 == d, scales[d], scale)

    feat_h[...] = features(th[:, 0, :] / scale, LOG2E, True).astype(BF16)
    eye = jnp.where(
        lax.broadcasted_iota(jnp.int32, (BLK, BLK), 0) == lax.broadcasted_iota(jnp.int32, (BLK, BLK), 1), -1.0, 0.0
    )
    for r in range(ROUNDS):
        cols = pl.ds(r * BLK, BLK)
        feat_s[:, cols] = features(tv[:, r, :] / scale, LOG2E, True).astype(BF16)
        lower = pv[r, pl.ds(0, BLK), :]
        upper = pv[r, pl.ds(BLK, BLK), :]
        if r == 0:
            lower = jnp.where(is_src, jnp.where(c == 0, eye, 0.0), lower)
            upper = jnp.where(is_src, jnp.where(c == 1, eye, 0.0), upper)
        p0f[:, cols] = lower
        h, l = parts2(upper)
        p1[pl.ds(0, BLK), cols] = h
        p1[pl.ds(BLK, BLK), cols] = h
        p1[pl.ds(2 * BLK, BLK), cols] = l

    for k in range(NZ):
        o = (z + k) % NZ
        if k:
            remote(group, gathered.at[o], sb.at[k], rb.at[o], in_line(k)).wait_recv()
        feats = features(gathered[o] / scale, 1.0, False)
        feat_t[pl.ds(pl.multiple_of(o * CHUNK, CHUNK), CHUNK), :] = feats.T.astype(BF16)

    def head_chunk(i, _):
        rows = pl.ds(pl.multiple_of(i * CHUNK, CHUNK), CHUNK)
        block = jnp.exp2(dot(feat_t[rows, :], feat_h[...]))
        a0[rows, :] = wide(block[:, :BLK])
        a1[rows, :] = wide(block[:, BLK:])
        return 0

    lax.fori_loop(0, NZ, head_chunk, 0)

    def pass_v():
        @pl.when(jnp.logical_not(is_src))
        def _():
            remote(vsrc.at[my_rows], gv.at[c, my_rows], sv1.at[0], rv1, plane(1)).wait_recv()

        @pl.when(is_src)
        def _():
            gv[c, my_rows, :] = vsrc[my_rows, :]

        for k in range(1, 8):
            send_v2(k).start()

    def pass_u():
        @pl.when(jnp.logical_not(is_src))
        def _():
            remote(usrc.at[my_rows], gu.at[my_rows], su1.at[0], ru1, plane(1)).wait_recv()

        @pl.when(is_src)
        def _():
            gu[my_rows, :] = usrc[my_rows, :]

        for k in range(1, 8):
            send_u2(k).start()

    @pl.when(c == 1)
    def _():
        pass_v()

    keep = jnp.where(is_src, 0.0, 1.0)

    def local_chunk(i, _):
        rows = pl.ds(pl.multiple_of(i * CHUNK, CHUNK), CHUNK)
        block = jnp.exp2(dot(feat_t[rows, :], feat_s[...]))
        acc[rows, pl.ds(0, BLK)] = block[:, :BLK] * keep
        acc[rows, pl.ds(BLK, COLS - BLK)] = block[:, BLK:]
        return 0

    lax.fori_loop(0, NZ, local_chunk, 0)

    @pl.when(c == 1)
    def _():
        pass_u()

    @pl.when(c == 0)
    def _():
        pass_v()

    def wait_v(cc):
        for k in range(NX):
            rows = pl.ds(k * PIECE, PIECE)

            @pl.when(jnp.logical_or(x != k, c != cc))
            def _():
                remote(gv.at[cc, rows], gv.at[cc, rows], sv2.at[0], rv2.at[cc, k], in_cross(1)).wait_recv()

    def wait_u():
        for k in range(NX):
            rows = pl.ds(k * PIECE, PIECE)

            @pl.when(jnp.logical_or(x != k, c != 1))
            def _():
                remote(gu.at[rows], gu.at[rows], su2.at[0], ru2.at[k], in_cross(1)).wait_recv()

    def stack(ref, value):
        h, l = parts2(value)
        ref[pl.ds(0, BLK), :] = h
        ref[pl.ds(BLK, BLK), :] = h
        ref[pl.ds(2 * BLK, BLK), :] = l

    wait_v(1)
    stack(w1, dot(wide(unpack_tri(gv[1])), p1[...]))

    def main_chunk(i, _):
        rows = pl.ds(pl.multiple_of(i * CHUNK, CHUNK), CHUNK)
        acc[rows, :] = acc[rows, :] - dot(a1[rows, :], w1[...])
        return 0

    lax.fori_loop(0, NZ, main_chunk, 0)

    wait_u()
    u01 = jnp.concatenate([gu[:, :BLK], gu[:, BLK:]], axis=0)
    stack(p0, p0f[...] - dot(wide(u01), w1[...]))
    wait_v(0)
    stack(w0, dot(wide(unpack_tri(gv[0])), p0[...]))

    for k in range(1, 8):
        send_a(k).wait_send()
        send_b(k).wait_send()
        send_v2(k).wait_send()

    @pl.when(c == 1)
    def _():
        for k in range(1, 8):
            send_u2(k).wait_send()

    @pl.when(is_src)
    def _():
        for k in range(1, 32):
            send_v1(k).wait_send()

    @pl.when(is_src & (c == 1))
    def _():
        for k in range(1, 32):
            send_u1(k).wait_send()


def finish_kernel(acc, a0, w0, out):
    rows = pl.ds(pl.multiple_of(pl.program_id(0) * CHUNK, CHUNK), CHUNK)
    block = acc[rows, :] - dot(a0[rows, :], w0[...])
    for r in range(ROUNDS):
        out[r] = block[:, r * BLK:(r + 1) * BLK]


def per_device(train_points, length_scales, test_points, lower_panel):
    vmem = pl.BlockSpec(memory_space=pltpu.VMEM)
    dma = pltpu.SemaphoreType.DMA
    acc, a0, w0 = pl.pallas_call(
        gather_kernel,
        out_shape=(
            pltpu.VMEM((TESTS, COLS), F32),
            pltpu.VMEM((TESTS, 3 * BLK), BF16),
            pltpu.VMEM((3 * BLK, COLS), BF16),
        ),
        in_specs=[pl.BlockSpec(memory_space=pltpu.HBM)] * 4,
        out_specs=(vmem, vmem, vmem),
        scratch_shapes=[
            pltpu.VMEM((DIM, 1, 32), F32),
            pltpu.SMEM((DIM,), F32),
            pltpu.VMEM((ROUNDS, 2 * BLK, BLK), F32),
            pltpu.VMEM((DIM, ROUNDS, BLK), F32),
            pltpu.VMEM((DIM, ROUNDS, 2 * BLK), F32),
            pltpu.VMEM((DIM, 128), F32),
            pltpu.VMEM((8, DIM, 128), F32),
            pltpu.VMEM((DIM, CHUNK), F32),
            pltpu.VMEM((NZ, DIM, CHUNK), F32),
            pltpu.VMEM((TESTS, FEAT), BF16),
            pltpu.VMEM((FEAT, COLS), BF16),
            pltpu.VMEM((FEAT, 2 * BLK), BF16),
            pltpu.VMEM((TESTS, 3 * BLK), BF16),
            pltpu.VMEM((3 * BLK, COLS), BF16),
            pltpu.VMEM((3 * BLK, COLS), BF16),
            pltpu.VMEM((3 * BLK, COLS), BF16),
            pltpu.VMEM((BLK, COLS), F32),
            pltpu.VMEM((HALF, TRI), F32),
            pltpu.VMEM((HALF, SQ), F32),
            pltpu.VMEM((2, HALF, TRI), F32),
            pltpu.VMEM((HALF, SQ), F32),
            dma((6,)),
            dma((8,)), dma((8,)), dma((8,)), dma((8,)),
            dma((32,)), dma, dma((32,)), dma,
            dma((8,)), dma((2, NX)), dma((8,)), dma((NX,)),
        ],
        compiler_params=pltpu.CompilerParams(
            collective_id=0, has_side_effects=True, vmem_limit_bytes=32 * 1024 * 1024
        ),
        name="gather_and_half",
    )(*(pltpu.with_memory_space_constraint(a, pltpu.HBM) for a in (train_points, length_scales, test_points, lower_panel)))
    return pl.pallas_call(
        finish_kernel,
        grid=(TESTS // CHUNK,),
        out_shape=jax.ShapeDtypeStruct((ROUNDS, TESTS, BLK), F32),
        in_specs=[vmem, vmem, vmem],
        out_specs=pl.BlockSpec((ROUNDS, CHUNK, BLK), lambda i: (0, i, 0)),
        compiler_params=pltpu.CompilerParams(vmem_limit_bytes=24 * 1024 * 1024),
        name="finish",
    )(acc, a0, w0)


def solution(mesh):
    placed = (P(), P(), P(None, "cols", "rows"), P(None, None, "rows"))
    return jax.shard_map(
        per_device, mesh=mesh, in_specs=placed, out_specs=P(None, "cols", "rows"), check_vma=False
    )
```

time: 552 us -> 54.2 us (0.10)
  the two profiles are of different devices: /device:TPU:37 before, /device:TPU:153 now
where the time goes in v1:
time: 54.2 us; the launch traced here: 54.1 us
  Pallas kernels  54.1 us (100%)
    pallas_call x1, Pallas kernels, per_device(): pl.pallas_call(gather_kernel, out_shape=(pltpu.VMEM((TESTS, COLS), F32),...  47.3 us
    pallas_call x1, Pallas kernels, per_device(): pl.pallas_call(finish_kernel, grid=(TESTS // CHUNK,), out_shape=jax.Shape...  6.79 us

profile of v1, /device:TPU:153, one launch (start us, length us, event | category | flops | bytes accessed | tf_op | source)
XLA Modules:
  0.0 54.1 jit_solution(4981702702451005299)
XLA Ops:
  0.0 47.3 %gather_and_half.1 = (f32[2048,1024]{1,0:T(8,128)S(1)}, bf16[2048,768]{1,0:T(8,128)(2,1)S(1)}, bf16[768,1024]{1,0:T(8,128)(2,1)S(1)}) custom-call(f32[8,4,16384]{2,1,0:T(4,128)} %train.1, f32[8]{0:T(128)} %scales_hbm.1, f32[8,1,32]{2,1,0:T(1,128)} %tests_hbm.1, f32[4,512,256]{2,1,0:T(8,128)} %panel.1), custom_call_target="tpu_custom_call" | custom-call | tf_op jit(solution)/shard_map/gather_and_half/pallas_call | solution.py:377
  47.3 6.8 %finish.1 = f32[4,2048,256]{2,1,0:T(8,128)} custom-call(f32[2048,1024]{1,0:T(8,128)S(1)} %get-tuple-element.8.acc, bf16[2048,768]{1,0:T(8,128)(2,1)S(1)} %get-tuple-element.9.a0, bf16[768,1024]{1,0:T(8,128)(2,1)S(1)} %get-tuple-element.10.w0), custom_call_target="tpu_custom_call" | custom-call | tf_op jit(solution)/shard_map/finish/pallas_call | solution.py:418

commit v2 on v1

--- a/solution.py
+++ b/solution.py
@@ -19,6 +19,7 @@
 DIM = 8
 TESTS = 2048
 CHUNK = TESTS // NZ
+TALL = TESTS // 2
 COLS = ROUNDS * BLK
 FEAT = 64
 PIECE = HALF // NX
@@ -95,7 +96,7 @@
     train, scales_hbm, tests_hbm, panel, acc, a0, w0,
     tests, scales, pv, tv, th, tile, slots, group, gathered, feat_t, feat_s, feat_h, a1, w1, p0, p1, p0f,
     vsrc, usrc, gv, gu,
-    lsem, sa, ra, sb, rb, sv1, rv1, su1, ru1, sv2, rv2, su2, ru2,
+    lsem, sa, ra, sb, rb, svy, svz, rv1, suy, suz, ru1, svx, rvx, sux, rux, line_ready,
 ):
     m = lax.axis_index("rows")
     x = lax.axis_index("cols")
@@ -130,13 +131,12 @@
         copy.start()
 
     barrier = pltpu.get_barrier_semaphore()
+    is_deputy = (m == 2) | (m == 3)
     for k in range(1, 8):
-        for who in (in_group(k), in_line(k), in_cross(k)):
+        line = (z + k) % NZ
+        deputy = jnp.where((line == 0) & (y == 0), 1, y)
+        for who in (in_group(k), in_cross(k), at(line, deputy, c, x)):
             pl.semaphore_signal(barrier, inc=1, device_id=who, device_id_type=MESH)
-
-    @pl.when(jnp.logical_not(is_src))
-    def _():
-        pl.semaphore_signal(barrier, inc=1, device_id=(c, x), device_id_type=MESH)
 
     tile[...] = jnp.zeros((DIM, 128), F32)
     load_tests.wait()
@@ -152,13 +152,11 @@
         vsrc[...] = jnp.concatenate([v[:HALF, :], v[HALF:, HALF:]], axis=1)
         usrc[...] = jnp.concatenate([pv[0, pl.ds(0, HALF), :], pv[0, pl.ds(HALF, HALF), :]], axis=1)
 
-    @pl.when(is_src)
-    def _():
-        pl.semaphore_wait(barrier, 21 + 31)
-
-    @pl.when(jnp.logical_not(is_src))
-    def _():
-        pl.semaphore_wait(barrier, 21)
+    pl.semaphore_wait(barrier, jnp.where(is_src, 14, jnp.where(is_deputy, 28, 21)))
+
+    @pl.when(is_deputy)
+    def _():
+        pl.semaphore_signal(line_ready, inc=1, device_id=(c, x), device_id_type=MESH)
 
     def remote(src, dst, ssem, rsem, who):
         return pltpu.make_async_remote_copy(
@@ -171,28 +169,49 @@
     def send_b(k):
         return remote(group, gathered.at[z], sb.at[k], rb.at[z], in_line(k))
 
-    def plane(k):
-        return at(k // NY, k % NY, c, x)
-
-    def send_v1(k):
-        return remote(vsrc.at[my_rows], gv.at[c, my_rows], sv1.at[k], rv1, plane(k))
-
-    def send_u1(k):
-        return remote(usrc.at[my_rows], gu.at[my_rows], su1.at[k], ru1, plane(k))
-
-    def send_v2(k):
-        return remote(gv.at[c, my_rows], gv.at[c, my_rows], sv2.at[k], rv2.at[c, x], in_cross(k))
-
-    def send_u2(k):
-        return remote(gu.at[my_rows], gu.at[my_rows], su2.at[k], ru2.at[x], in_cross(k))
-
-    for k in range(1, 8):
-        send_a(k).start()
+    def send_vy(k):
+        return remote(vsrc.at[my_rows], gv.at[c, my_rows], svy.at[k], rv1, at(0, k, c, x))
+
+    def send_uy(k):
+        return remote(usrc.at[my_rows], gu.at[my_rows], suy.at[k], ru1, at(0, k, c, x))
+
+    def send_vz(k):
+        return remote(gv.at[c, my_rows], gv.at[c, my_rows], svz.at[k], rv1, at(k, y, c, x))
+
+    def send_uz(k):
+        return remote(gu.at[my_rows], gu.at[my_rows], suz.at[k], ru1, at(k, y, c, x))
+
+    def send_vx(k):
+        return remote(gv.at[c, my_rows], gv.at[c, my_rows], svx.at[k], rvx.at[c, x], in_cross(k))
+
+    def send_ux(k):
+        return remote(gu.at[my_rows], gu.at[my_rows], sux.at[k], rux.at[x], in_cross(k))
+
+    def start(send, count):
+        for k in range(1, count):
+            send(k).start()
+
+    not_src = jnp.logical_not(is_src)
+    start(send_a, 8)
+
+    @pl.when(is_src)
+    def _():
+        start(send_vy, NY)
+        gv[c, my_rows, :] = vsrc[my_rows, :]
 
     @pl.when(is_src & (c == 1))
     def _():
-        for k in range(1, 32):
-            send_v1(k).start()
+        start(send_uy, NY)
+        gu[my_rows, :] = usrc[my_rows, :]
+
+    @pl.when((z == 0) & (c == 1) & not_src)
+    def _():
+        send_vy(1).wait_recv()
+        start(send_vz, NZ)
+
+    @pl.when((z == 0) & (c == 1))
+    def _():
+        start(send_vx, 8)
 
     slots[q] = tile[...]
     for k in range(1, 8):
@@ -203,19 +222,35 @@
         for j in range(1, 4):
             total = total + pltpu.roll(slots[4 * h + j], 32 * j, 1)
         group[:, pl.ds(128 * h, 128)] = total
-    for k in range(1, 8):
-        send_b(k).start()
+
+    @pl.when(is_src)
+    def _():
+        pl.semaphore_wait(line_ready, 1)
+
+    @pl.when(is_src & (c == 1))
+    def _():
+        start(send_vz, NZ)
+
+    start(send_b, 8)
     gathered[z] = group[...]
 
-    @pl.when(is_src & (c == 1))
-    def _():
-        for k in range(1, 32):
-            send_u1(k).start()
-
-    @pl.when(is_src & (c == 0))
-    def _():
-        for k in range(1, 32):
-            send_v1(k).start()
+    @pl.when((z == 0) & (c == 1) & not_src)
+    def _():
+        send_uy(1).wait_recv()
+
+    @pl.when((z == 0) & (c == 1))
+    def _():
+        start(send_uz, NZ)
+        start(send_ux, 8)
+
+    @pl.when((z == 0) & (c == 0) & not_src)
+    def _():
+        send_vy(1).wait_recv()
+
+    @pl.when((z == 0) & (c == 0))
+    def _():
+        start(send_vz, NZ)
+        start(send_vx, 8)
 
     for copy in loads[1:]:
         copy.wait()
@@ -242,12 +277,17 @@
         p1[pl.ds(BLK, BLK), cols] = h
         p1[pl.ds(2 * BLK, BLK), cols] = l
 
-    for k in range(NZ):
-        o = (z + k) % NZ
-        if k:
-            remote(group, gathered.at[o], sb.at[k], rb.at[o], in_line(k)).wait_recv()
-        feats = features(gathered[o] / scale, 1.0, False)
-        feat_t[pl.ds(pl.multiple_of(o * CHUNK, CHUNK), CHUNK), :] = feats.T.astype(BF16)
+    @pl.when((z > 0) & (c == 1))
+    def _():
+        send_vy(1).wait_recv()
+        start(send_vx, 8)
+
+    for o in range(NZ):
+        @pl.when(z != o)
+        def _():
+            remote(group, gathered.at[o], sb.at[0], rb.at[o], in_line(1)).wait_recv()
+
+        feat_t[pl.ds(o * CHUNK, CHUNK), :] = features(gathered[o] / scale, 1.0, False).T.astype(BF16)
 
     def head_chunk(i, _):
         rows = pl.ds(pl.multiple_of(i * CHUNK, CHUNK), CHUNK)
@@ -258,33 +298,15 @@
 
     lax.fori_loop(0, NZ, head_chunk, 0)
 
-    def pass_v():
-        @pl.when(jnp.logical_not(is_src))
-        def _():
-            remote(vsrc.at[my_rows], gv.at[c, my_rows], sv1.at[0], rv1, plane(1)).wait_recv()
-
-        @pl.when(is_src)
-        def _():
-            gv[c, my_rows, :] = vsrc[my_rows, :]
-
-        for k in range(1, 8):
-            send_v2(k).start()
-
-    def pass_u():
-        @pl.when(jnp.logical_not(is_src))
-        def _():
-            remote(usrc.at[my_rows], gu.at[my_rows], su1.at[0], ru1, plane(1)).wait_recv()
-
-        @pl.when(is_src)
-        def _():
-            gu[my_rows, :] = usrc[my_rows, :]
-
-        for k in range(1, 8):
-            send_u2(k).start()
-
-    @pl.when(c == 1)
-    def _():
-        pass_v()
+    @pl.when((z > 0) & (c == 1))
+    def _():
+        send_uy(1).wait_recv()
+        start(send_ux, 8)
+
+    @pl.when((z > 0) & (c == 0))
+    def _():
+        send_vy(1).wait_recv()
+        start(send_vx, 8)
 
     keep = jnp.where(is_src, 0.0, 1.0)
 
@@ -297,21 +319,13 @@
 
     lax.fori_loop(0, NZ, local_chunk, 0)
 
-    @pl.when(c == 1)
-    def _():
-        pass_u()
-
-    @pl.when(c == 0)
-    def _():
-        pass_v()
-
     def wait_v(cc):
         for k in range(NX):
             rows = pl.ds(k * PIECE, PIECE)
 
             @pl.when(jnp.logical_or(x != k, c != cc))
             def _():
-                remote(gv.at[cc, rows], gv.at[cc, rows], sv2.at[0], rv2.at[cc, k], in_cross(1)).wait_recv()
+                remote(gv.at[cc, rows], gv.at[cc, rows], svx.at[0], rvx.at[cc, k], in_cross(1)).wait_recv()
 
     def wait_u():
         for k in range(NX):
@@ -319,7 +333,7 @@
 
             @pl.when(jnp.logical_or(x != k, c != 1))
             def _():
-                remote(gu.at[rows], gu.at[rows], su2.at[0], ru2.at[k], in_cross(1)).wait_recv()
+                remote(gu.at[rows], gu.at[rows], sux.at[0], rux.at[k], in_cross(1)).wait_recv()
 
     def stack(ref, value):
         h, l = parts2(value)
@@ -331,11 +345,12 @@
     stack(w1, dot(wide(unpack_tri(gv[1])), p1[...]))
 
     def main_chunk(i, _):
-        rows = pl.ds(pl.multiple_of(i * CHUNK, CHUNK), CHUNK)
-        acc[rows, :] = acc[rows, :] - dot(a1[rows, :], w1[...])
+        rows = pl.ds(pl.multiple_of((i % 2) * TALL, TALL), TALL)
+        cols = pl.ds(pl.multiple_of((i // 2) * BLK, BLK), BLK)
+        acc[rows, cols] = acc[rows, cols] - dot(a1[rows, :], w1[:, cols])
         return 0
 
-    lax.fori_loop(0, NZ, main_chunk, 0)
+    lax.fori_loop(0, 2 * ROUNDS, main_chunk, 0)
 
     wait_u()
     u01 = jnp.concatenate([gu[:, :BLK], gu[:, BLK:]], axis=0)
@@ -343,29 +358,36 @@
     wait_v(0)
     stack(w0, dot(wide(unpack_tri(gv[0])), p0[...]))
 
-    for k in range(1, 8):
-        send_a(k).wait_send()
-        send_b(k).wait_send()
-        send_v2(k).wait_send()
+    def sent(send, count):
+        for k in range(1, count):
+            send(k).wait_send()
+
+    for send in (send_a, send_b, send_vx):
+        sent(send, 8)
+
+    @pl.when(z == 0)
+    def _():
+        sent(send_vz, NZ)
 
     @pl.when(c == 1)
     def _():
-        for k in range(1, 8):
-            send_u2(k).wait_send()
+        sent(send_ux, 8)
+
+    @pl.when((z == 0) & (c == 1))
+    def _():
+        sent(send_uz, NZ)
 
     @pl.when(is_src)
     def _():
-        for k in range(1, 32):
-            send_v1(k).wait_send()
+        sent(send_vy, NY)
 
     @pl.when(is_src & (c == 1))
     def _():
-        for k in range(1, 32):
-            send_u1(k).wait_send()
+        sent(send_uy, NY)
 
 
 def finish_kernel(acc, a0, w0, out):
-    rows = pl.ds(pl.multiple_of(pl.program_id(0) * CHUNK, CHUNK), CHUNK)
+    rows = pl.ds(pl.multiple_of(pl.program_id(0) * (TESTS // 4), TESTS // 4), TESTS // 4)
     block = acc[rows, :] - dot(a0[rows, :], w0[...])
     for r in range(ROUNDS):
         out[r] = block[:, r * BLK:(r + 1) * BLK]
@@ -407,8 +429,9 @@
             pltpu.VMEM((HALF, SQ), F32),
             dma((6,)),
             dma((8,)), dma((8,)), dma((8,)), dma((8,)),
-            dma((32,)), dma, dma((32,)), dma,
+            dma((NY,)), dma((NZ,)), dma, dma((NY,)), dma((NZ,)), dma,
             dma((8,)), dma((2, NX)), dma((8,)), dma((NX,)),
+            pltpu.SemaphoreType.REGULAR,
         ],
         compiler_params=pltpu.CompilerParams(
             collective_id=0, has_side_effects=True, vmem_limit_bytes=32 * 1024 * 1024
@@ -417,10 +440,10 @@
     )(*(pltpu.with_memory_space_constraint(a, pltpu.HBM) for a in (train_points, length_scales, test_points, lower_panel)))
     return pl.pallas_call(
         finish_kernel,
-        grid=(TESTS // CHUNK,),
+        grid=(4,),
         out_shape=jax.ShapeDtypeStruct((ROUNDS, TESTS, BLK), F32),
         in_specs=[vmem, vmem, vmem],
-        out_specs=pl.BlockSpec((ROUNDS, CHUNK, BLK), lambda i: (0, i, 0)),
+        out_specs=pl.BlockSpec((ROUNDS, TESTS // 4, BLK), lambda i: (0, i, 0)),
         compiler_params=pltpu.CompilerParams(vmem_limit_bytes=24 * 1024 * 1024),
         name="finish",
     )(acc, a0, w0)

time: 54.2 us -> 36.9 us (0.68)
  the two profiles are of different devices: /device:TPU:153 before, /device:TPU:37 now
where the time goes in v2:
time: 36.9 us; the launch traced here: 36.8 us
  Pallas kernels  36.8 us (100%)
    pallas_call x1, Pallas kernels, per_device(): pl.pallas_call(gather_kernel, out_shape=(pltpu.VMEM((TESTS, COLS), F32),...  31.1 us
    pallas_call x1, Pallas kernels, per_device(): pl.pallas_call(finish_kernel, grid=(4,), out_shape=jax.ShapeDtypeStruct((...  5.62 us

profile of v2, /device:TPU:37, one launch (start us, length us, event | category | flops | bytes accessed | tf_op | source)
XLA Modules:
  0.0 36.8 jit_solution(17841216170600585421)
XLA Ops:
  0.0 31.1 %gather_and_half.1 = (f32[2048,1024]{1,0:T(8,128)S(1)}, bf16[2048,768]{1,0:T(8,128)(2,1)S(1)}, bf16[768,1024]{1,0:T(8,128)(2,1)S(1)}) custom-call(f32[8,4,16384]{2,1,0:T(4,128)} %train.1, f32[8]{0:T(128)} %scales_hbm.1, f32[8,1,32]{2,1,0:T(1,128)} %tests_hbm.1, f32[4,512,256]{2,1,0:T(8,128)} %panel.1), custom_call_target="tpu_custom_call" | custom-call | tf_op jit(solution)/shard_map/gather_and_half/pallas_call | solution.py:399
  31.1 5.6 %finish.1 = f32[4,2048,256]{2,1,0:T(8,128)} custom-call(f32[2048,1024]{1,0:T(8,128)S(1)} %get-tuple-element.8.acc, bf16[2048,768]{1,0:T(8,128)(2,1)S(1)} %get-tuple-element.9.a0, bf16[768,1024]{1,0:T(8,128)(2,1)S(1)} %get-tuple-element.10.w0), custom_call_target="tpu_custom_call" | custom-call | tf_op jit(solution)/shard_map/finish/pallas_call | solution.py:441

commit v3 on v2

--- a/solution.py
+++ b/solution.py
@@ -20,6 +20,7 @@
 TESTS = 2048
 CHUNK = TESTS // NZ
 TALL = TESTS // 2
+TILE = TESTS // 8
 COLS = ROUNDS * BLK
 FEAT = 64
 PIECE = HALF // NX
@@ -69,22 +70,26 @@
 def upper_inverse(u):
     row = lax.broadcasted_iota(jnp.int32, (BLK, BLK), 0)
     col = lax.broadcasted_iota(jnp.int32, (BLK, BLK), 1)
-    eye = row == col
-    on_diag = jnp.where(eye, u, 0.0)
+    on_diag = jnp.where(row == col, u, 0.0)
     d_col = jnp.sum(on_diag, axis=1, keepdims=True)
     d_row = jnp.sum(on_diag, axis=0, keepdims=True)
     strict = jnp.where(col > row, u, 0.0) / d_col
+    row, col = row[:HALF, :HALF], col[:HALF, :HALF]
+    blocks = [strict[:HALF, :HALF], strict[HALF:, HALF:]]
     size = 32
-    power = jnp.where(row // size == col // size, -strict, 0.0)
-    inverse = jnp.where(eye, 1.0, 0.0) + power
+    powers = [jnp.where(row // size == col // size, -n, 0.0) for n in blocks]
+    inverses = [jnp.where(row == col, 1.0, 0.0) + p for p in powers]
     for _ in range(4):
-        power = dot_full(power, power)
-        inverse = inverse + dot_full(inverse, power)
-    while size < BLK:
+        powers = [dot_full(p, p) for p in powers]
+        inverses = [v + dot_full(v, p) for v, p in zip(inverses, powers)]
+    while size < HALF:
         pair = (row // (2 * size) == col // (2 * size)) & (row // size != col // size)
-        inverse = inverse - dot_full(dot_full(inverse, jnp.where(pair, strict, 0.0)), inverse)
+        halves = [dot_full(v, jnp.where(pair, n, 0.0)) for v, n in zip(inverses, blocks)]
+        inverses = [v - dot_full(h, v) for v, h in zip(inverses, halves)]
         size *= 2
-    return inverse / d_row
+    corner = -dot_full(dot_full(inverses[0], strict[:HALF, HALF:]), inverses[1])
+    top = jnp.concatenate([inverses[0], corner], axis=1) / d_row
+    return jnp.concatenate([top, inverses[1] / d_row[:, HALF:]], axis=1)
 
 
 def unpack_tri(packed):
@@ -147,9 +152,7 @@
 
     @pl.when(is_src)
     def _():
-        u = pv[0, pl.ds(pl.multiple_of(c * BLK, BLK), BLK), :]
-        v = upper_inverse(u)
-        vsrc[...] = jnp.concatenate([v[:HALF, :], v[HALF:, HALF:]], axis=1)
+        vsrc[...] = upper_inverse(pv[0, pl.ds(pl.multiple_of(c * BLK, BLK), BLK), :])
         usrc[...] = jnp.concatenate([pv[0, pl.ds(0, HALF), :], pv[0, pl.ds(HALF, HALF), :]], axis=1)
 
     pl.semaphore_wait(barrier, jnp.where(is_src, 14, jnp.where(is_deputy, 28, 21)))
@@ -204,14 +207,27 @@
         start(send_uy, NY)
         gu[my_rows, :] = usrc[my_rows, :]
 
+    @pl.when(is_src)
+    def _():
+        pl.semaphore_wait(line_ready, 1)
+
     @pl.when((z == 0) & (c == 1) & not_src)
     def _():
         send_vy(1).wait_recv()
+
+    @pl.when((z == 0) & (c == 1))
+    def _():
         start(send_vz, NZ)
+        start(send_vx, 8)
+
+    @pl.when((z == 0) & (c == 1) & not_src)
+    def _():
+        send_uy(1).wait_recv()
 
     @pl.when((z == 0) & (c == 1))
     def _():
-        start(send_vx, 8)
+        start(send_uz, NZ)
+        start(send_ux, 8)
 
     slots[q] = tile[...]
     for k in range(1, 8):
@@ -223,25 +239,8 @@
             total = total + pltpu.roll(slots[4 * h + j], 32 * j, 1)
         group[:, pl.ds(128 * h, 128)] = total
 
-    @pl.when(is_src)
-    def _():
-        pl.semaphore_wait(line_ready, 1)
-
-    @pl.when(is_src & (c == 1))
-    def _():
-        start(send_vz, NZ)
-
     start(send_b, 8)
     gathered[z] = group[...]
-
-    @pl.when((z == 0) & (c == 1) & not_src)
-    def _():
-        send_uy(1).wait_recv()
-
-    @pl.when((z == 0) & (c == 1))
-    def _():
-        start(send_uz, NZ)
-        start(send_ux, 8)
 
     @pl.when((z == 0) & (c == 0) & not_src)
     def _():
@@ -277,48 +276,6 @@
         p1[pl.ds(BLK, BLK), cols] = h
         p1[pl.ds(2 * BLK, BLK), cols] = l
 
-    @pl.when((z > 0) & (c == 1))
-    def _():
-        send_vy(1).wait_recv()
-        start(send_vx, 8)
-
-    for o in range(NZ):
-        @pl.when(z != o)
-        def _():
-            remote(group, gathered.at[o], sb.at[0], rb.at[o], in_line(1)).wait_recv()
-
-        feat_t[pl.ds(o * CHUNK, CHUNK), :] = features(gathered[o] / scale, 1.0, False).T.astype(BF16)
-
-    def head_chunk(i, _):
-        rows = pl.ds(pl.multiple_of(i * CHUNK, CHUNK), CHUNK)
-        block = jnp.exp2(dot(feat_t[rows, :], feat_h[...]))
-        a0[rows, :] = wide(block[:, :BLK])
-        a1[rows, :] = wide(block[:, BLK:])
-        return 0
-
-    lax.fori_loop(0, NZ, head_chunk, 0)
-
-    @pl.when((z > 0) & (c == 1))
-    def _():
-        send_uy(1).wait_recv()
-        start(send_ux, 8)
-
-    @pl.when((z > 0) & (c == 0))
-    def _():
-        send_vy(1).wait_recv()
-        start(send_vx, 8)
-
-    keep = jnp.where(is_src, 0.0, 1.0)
-
-    def local_chunk(i, _):
-        rows = pl.ds(pl.multiple_of(i * CHUNK, CHUNK), CHUNK)
-        block = jnp.exp2(dot(feat_t[rows, :], feat_s[...]))
-        acc[rows, pl.ds(0, BLK)] = block[:, :BLK] * keep
-        acc[rows, pl.ds(BLK, COLS - BLK)] = block[:, BLK:]
-        return 0
-
-    lax.fori_loop(0, NZ, local_chunk, 0)
-
     def wait_v(cc):
         for k in range(NX):
             rows = pl.ds(k * PIECE, PIECE)
@@ -341,22 +298,58 @@
         ref[pl.ds(BLK, BLK), :] = h
         ref[pl.ds(2 * BLK, BLK), :] = l
 
-    wait_v(1)
-    stack(w1, dot(wide(unpack_tri(gv[1])), p1[...]))
+    def first_weights():
+        wait_v(1)
+        stack(w1, dot(wide(unpack_tri(gv[1])), p1[...]))
+
+    def second_weights():
+        wait_u()
+        u01 = jnp.concatenate([gu[:, :BLK], gu[:, BLK:]], axis=0)
+        stack(p0, p0f[...] - dot(wide(u01), w1[...]))
+        wait_v(0)
+        stack(w0, dot(wide(unpack_tri(gv[0])), p0[...]))
+
+    keep = jnp.where(is_src, 0.0, 1.0)
+
+    def covariance(half):
+        for o in range(half * NZ // 2, (half + 1) * NZ // 2):
+            @pl.when(z != o)
+            def _():
+                remote(group, gathered.at[o], sb.at[0], rb.at[o], in_line(1)).wait_recv()
+
+            feat_t[pl.ds(o * CHUNK, CHUNK), :] = features(gathered[o] / scale, 1.0, False).T.astype(BF16)
+        rows = pl.ds(half * TALL, TALL)
+        block = jnp.exp2(dot(feat_t[rows, :], feat_h[...]))
+        a0[rows, :] = wide(block[:, :BLK])
+        a1[rows, :] = wide(block[:, BLK:])
+        block = jnp.exp2(dot(feat_t[rows, :], feat_s[...]))
+        acc[rows, pl.ds(0, BLK)] = block[:, :BLK] * keep
+        acc[rows, pl.ds(BLK, COLS - BLK)] = block[:, BLK:]
 
     def main_chunk(i, _):
-        rows = pl.ds(pl.multiple_of((i % 2) * TALL, TALL), TALL)
-        cols = pl.ds(pl.multiple_of((i // 2) * BLK, BLK), BLK)
-        acc[rows, cols] = acc[rows, cols] - dot(a1[rows, :], w1[:, cols])
+        rows = pl.ds(pl.multiple_of(i * TALL, TALL), TALL)
+        acc[rows, :] = acc[rows, :] - dot(a1[rows, :], w1[...])
         return 0
 
-    lax.fori_loop(0, 2 * ROUNDS, main_chunk, 0)
-
-    wait_u()
-    u01 = jnp.concatenate([gu[:, :BLK], gu[:, BLK:]], axis=0)
-    stack(p0, p0f[...] - dot(wide(u01), w1[...]))
-    wait_v(0)
-    stack(w0, dot(wide(unpack_tri(gv[0])), p0[...]))
+    @pl.when(z > 0)
+    def _():
+        send_vy(1).wait_recv()
+        start(send_vx, 8)
+
+    @pl.when((z > 0) & (c == 1))
+    def _():
+        send_uy(1).wait_recv()
+        start(send_ux, 8)
+
+    covariance(0)
+
+    covariance(1)
+
+    first_weights()
+
+    lax.fori_loop(0, TESTS // TALL, main_chunk, 0)
+
+    second_weights()
 
     def sent(send, count):
         for k in range(1, count):
@@ -386,11 +379,17 @@
         sent(send_uy, NY)
 
 
-def finish_kernel(acc, a0, w0, out):
-    rows = pl.ds(pl.multiple_of(pl.program_id(0) * (TESTS // 4), TESTS // 4), TESTS // 4)
-    block = acc[rows, :] - dot(a0[rows, :], w0[...])
-    for r in range(ROUNDS):
-        out[r] = block[:, r * BLK:(r + 1) * BLK]
+def finish_kernel(acc, a0, w0, out, done, sem):
+    copies = []
+    for i in range(TESTS // TILE):
+        rows = pl.ds(i * TILE, TILE)
+        block = acc[rows, :] - dot(a0[rows, :], w0[...])
+        for r in range(ROUNDS):
+            done[r, rows, :] = block[:, r * BLK:(r + 1) * BLK]
+            copies.append(pltpu.make_async_copy(done.at[r, rows], out.at[r, rows], sem.at[i * ROUNDS + r]))
+            copies[-1].start()
+    for copy in copies:
+        copy.wait()
 
 
 def per_device(train_points, length_scales, test_points, lower_panel):
@@ -440,10 +439,10 @@
     )(*(pltpu.with_memory_space_constraint(a, pltpu.HBM) for a in (train_points, length_scales, test_points, lower_panel)))
     return pl.pallas_call(
         finish_kernel,
-        grid=(4,),
         out_shape=jax.ShapeDtypeStruct((ROUNDS, TESTS, BLK), F32),
         in_specs=[vmem, vmem, vmem],
-        out_specs=pl.BlockSpec((ROUNDS, TESTS // 4, BLK), lambda i: (0, i, 0)),
+        out_specs=pl.BlockSpec(memory_space=pltpu.HBM),
+        scratch_shapes=[pltpu.VMEM((ROUNDS, TESTS, BLK), F32), dma((ROUNDS * TESTS // TILE,))],
         compiler_params=pltpu.CompilerParams(vmem_limit_bytes=24 * 1024 * 1024),
         name="finish",
     )(acc, a0, w0)

time: 36.9 us -> 30.4 us (0.82)
  the two profiles are of different devices: /device:TPU:37 before, /device:TPU:134 now
where the time goes in v3:
time: 30.4 us; the launch traced here: 30.3 us
  Pallas kernels  30.3 us (100%)
    pallas_call x1, Pallas kernels, per_device(): pl.pallas_call(gather_kernel, out_shape=(pltpu.VMEM((TESTS, COLS), F32),...  25.3 us
    pallas_call x1, Pallas kernels, per_device(): pl.pallas_call(finish_kernel, out_shape=jax.ShapeDtypeStruct((ROUNDS, TES...  4.96 us

profile of v3, /device:TPU:134, one launch (start us, length us, event | category | flops | bytes accessed | tf_op | source)
XLA Modules:
  0.0 30.3 jit_solution(9810997926934188404)
XLA Ops:
  0.0 25.3 %gather_and_half.1 = (f32[2048,1024]{1,0:T(8,128)S(1)}, bf16[2048,768]{1,0:T(8,128)(2,1)S(1)}, bf16[768,1024]{1,0:T(8,128)(2,1)S(1)}) custom-call(f32[8,4,16384]{2,1,0:T(4,128)} %train.1, f32[8]{0:T(128)} %scales_hbm.1, f32[8,1,32]{2,1,0:T(1,128)} %tests_hbm.1, f32[4,512,256]{2,1,0:T(8,128)} %panel.1), custom_call_target="tpu_custom_call" | custom-call | tf_op jit(solution)/shard_map/gather_and_half/pallas_call | solution.py:398
  25.3 5.0 %finish.1 = f32[4,2048,256]{2,1,0:T(8,128)} custom-call(f32[2048,1024]{1,0:T(8,128)S(1)} %get-tuple-element.8.acc, bf16[2048,768]{1,0:T(8,128)(2,1)S(1)} %get-tuple-element.9.a0, bf16[768,1024]{1,0:T(8,128)(2,1)S(1)} %get-tuple-element.10.w0), custom_call_target="tpu_custom_call" | custom-call | tf_op jit(solution)/shard_map/finish/pallas_call | solution.py:440

commit v4 on v3

--- a/solution.py
+++ b/solution.py
@@ -20,7 +20,8 @@
 TESTS = 2048
 CHUNK = TESTS // NZ
 TALL = TESTS // 2
-TILE = TESTS // 8
+SIZES = (1, 1, 2, 2, 1, 1)
+ARRIVAL = (0, 1, 7, 2, 6, 3, 5, 4)
 COLS = ROUNDS * BLK
 FEAT = 64
 PIECE = HALF // NX
@@ -312,12 +313,11 @@
     keep = jnp.where(is_src, 0.0, 1.0)
 
     def covariance(half):
-        for o in range(half * NZ // 2, (half + 1) * NZ // 2):
-            @pl.when(z != o)
-            def _():
+        for slot in range(half * NZ // 2, (half + 1) * NZ // 2):
+            o = (z + ARRIVAL[slot]) % NZ
+            if slot:
                 remote(group, gathered.at[o], sb.at[0], rb.at[o], in_line(1)).wait_recv()
-
-            feat_t[pl.ds(o * CHUNK, CHUNK), :] = features(gathered[o] / scale, 1.0, False).T.astype(BF16)
+            feat_t[pl.ds(slot * CHUNK, CHUNK), :] = features(gathered[o] / scale, 1.0, False).T.astype(BF16)
         rows = pl.ds(half * TALL, TALL)
         block = jnp.exp2(dot(feat_t[rows, :], feat_h[...]))
         a0[rows, :] = wide(block[:, :BLK])
@@ -326,12 +326,7 @@
         acc[rows, pl.ds(0, BLK)] = block[:, :BLK] * keep
         acc[rows, pl.ds(BLK, COLS - BLK)] = block[:, BLK:]
 
-    def main_chunk(i, _):
-        rows = pl.ds(pl.multiple_of(i * TALL, TALL), TALL)
-        acc[rows, :] = acc[rows, :] - dot(a1[rows, :], w1[...])
-        return 0
-
-    @pl.when(z > 0)
+    @pl.when((z > 0) & (c == 1))
     def _():
         send_vy(1).wait_recv()
         start(send_vx, 8)
@@ -341,13 +336,34 @@
         send_uy(1).wait_recv()
         start(send_ux, 8)
 
+    @pl.when(z == 0)
+    def _():
+        first_weights()
+
+    far = (z >= 3) & (z <= 5)
+    near = (z > 0) & jnp.logical_not(far)
     covariance(0)
 
+    @pl.when(near & (c == 0))
+    def _():
+        send_vy(1).wait_recv()
+        start(send_vx, 8)
+
+
     covariance(1)
 
-    first_weights()
-
-    lax.fori_loop(0, TESTS // TALL, main_chunk, 0)
+    @pl.when(far & (c == 0))
+    def _():
+        send_vy(1).wait_recv()
+        start(send_vx, 8)
+
+    @pl.when(z > 0)
+    def _():
+        first_weights()
+
+    for i in range(TESTS // TALL):
+        rows = pl.ds(i * TALL, TALL)
+        acc[rows, :] = acc[rows, :] - dot(a1[rows, :], w1[...])
 
     second_weights()
 
@@ -380,14 +396,21 @@
 
 
 def finish_kernel(acc, a0, w0, out, done, sem):
+    z = lax.axis_index("rows") // 8
     copies = []
-    for i in range(TESTS // TILE):
-        rows = pl.ds(i * TILE, TILE)
+    first = 0
+    for count in SIZES:
+        rows = pl.ds(first * CHUNK, count * CHUNK)
         block = acc[rows, :] - dot(a0[rows, :], w0[...])
         for r in range(ROUNDS):
             done[r, rows, :] = block[:, r * BLK:(r + 1) * BLK]
-            copies.append(pltpu.make_async_copy(done.at[r, rows], out.at[r, rows], sem.at[i * ROUNDS + r]))
-            copies[-1].start()
+        for i in range(first, first + count):
+            tests = pl.ds(pl.multiple_of((z + ARRIVAL[i]) % NZ * CHUNK, CHUNK), CHUNK)
+            for r in range(ROUNDS):
+                source = done.at[r, pl.ds(i * CHUNK, CHUNK)]
+                copies.append(pltpu.make_async_copy(source, out.at[r, tests], sem.at[i * ROUNDS + r]))
+                copies[-1].start()
+        first += count
     for copy in copies:
         copy.wait()
 
@@ -442,7 +465,7 @@
         out_shape=jax.ShapeDtypeStruct((ROUNDS, TESTS, BLK), F32),
         in_specs=[vmem, vmem, vmem],
         out_specs=pl.BlockSpec(memory_space=pltpu.HBM),
-        scratch_shapes=[pltpu.VMEM((ROUNDS, TESTS, BLK), F32), dma((ROUNDS * TESTS // TILE,))],
+        scratch_shapes=[pltpu.VMEM((ROUNDS, TESTS, BLK), F32), dma((ROUNDS * NZ,))],
         compiler_params=pltpu.CompilerParams(vmem_limit_bytes=24 * 1024 * 1024),
         name="finish",
     )(acc, a0, w0)

time: 30.4 us -> 29.7 us (0.977)
  the two profiles are of different devices: /device:TPU:134 before, /device:TPU:37 now
where the time goes in v4:
time: 29.7 us; the launch traced here: 29.6 us
  Pallas kernels  29.4 us (99%)
    pallas_call x1, Pallas kernels, per_device(): pl.pallas_call(gather_kernel, out_shape=(pltpu.VMEM((TESTS, COLS), F32),...  24.6 us
    pallas_call x1, Pallas kernels, per_device(): pl.pallas_call(finish_kernel, out_shape=jax.ShapeDtypeStruct((ROUNDS, TES...  4.78 us

profile of v4, /device:TPU:37, one launch (start us, length us, event | category | flops | bytes accessed | tf_op | source)
XLA Modules:
  0.0 29.6 jit_solution(941243422220060277)
XLA Ops:
  0.0 24.6 %gather_and_half.1 = (f32[2048,1024]{1,0:T(8,128)S(1)}, bf16[2048,768]{1,0:T(8,128)(2,1)S(1)}, bf16[768,1024]{1,0:T(8,128)(2,1)S(1)}) custom-call(f32[8,4,16384]{2,1,0:T(4,128)} %train.1, f32[8]{0:T(128)} %scales_hbm.1, f32[8,1,32]{2,1,0:T(1,128)} %tests_hbm.1, f32[4,512,256]{2,1,0:T(8,128)} %panel.1), custom_call_target="tpu_custom_call" | custom-call | tf_op jit(solution)/shard_map/gather_and_half/pallas_call | solution.py:421
  24.7 4.8 %finish.1 = f32[4,2048,256]{2,1,0:T(8,128)} custom-call(f32[2048,1024]{1,0:T(8,128)S(1)} %get-tuple-element.8.acc, bf16[2048,768]{1,0:T(8,128)(2,1)S(1)} %get-tuple-element.9.a0, bf16[768,1024]{1,0:T(8,128)(2,1)S(1)} %get-tuple-element.10.w0), custom_call_target="tpu_custom_call" | custom-call | tf_op jit(solution)/shard_map/finish/pallas_call | solution.py:463

commit v5 on v4

--- a/solution.py
+++ b/solution.py
@@ -25,7 +25,9 @@
 COLS = ROUNDS * BLK
 FEAT = 64
 PIECE = HALF // NX
-TRI = BLK + HALF
+STRIP = BLK // NX
+TRI = 10 * STRIP
+TRI_PIECE = STRIP // NX
 SQ = 2 * BLK
 
 
@@ -90,12 +92,22 @@
         size *= 2
     corner = -dot_full(dot_full(inverses[0], strict[:HALF, HALF:]), inverses[1])
     top = jnp.concatenate([inverses[0], corner], axis=1) / d_row
-    return jnp.concatenate([top, inverses[1] / d_row[:, HALF:]], axis=1)
+    low = jnp.concatenate([jnp.zeros((HALF, HALF), F32), inverses[1] / d_row[:, HALF:]], axis=1)
+    return jnp.concatenate([top, low], axis=0)
+
+
+def pack_tri(v):
+    return jnp.concatenate([v[k * STRIP:(k + 1) * STRIP, k * STRIP:] for k in range(NX)], axis=1)
 
 
 def unpack_tri(packed):
-    low = jnp.concatenate([jnp.zeros((HALF, HALF), F32), packed[:, BLK:]], axis=1)
-    return jnp.concatenate([packed[:, :BLK], low], axis=0)
+    strips, first = [packed[:, :BLK]], BLK
+    for k in range(1, NX):
+        width = BLK - k * STRIP
+        strip = packed[:, first:first + width]
+        strips.append(jnp.concatenate([jnp.zeros((STRIP, k * STRIP), F32), strip], axis=1))
+        first += width
+    return jnp.concatenate(strips, axis=0)
 
 
 def gather_kernel(
@@ -149,11 +161,12 @@
     tile[:, pl.ds(0, 32)] = tests[:, 0, :]
 
     my_rows = pl.ds(pl.multiple_of(x * PIECE, PIECE), PIECE)
+    tri_rows = pl.ds(pl.multiple_of(x * TRI_PIECE, TRI_PIECE), TRI_PIECE)
     loads[0].wait()
 
     @pl.when(is_src)
     def _():
-        vsrc[...] = upper_inverse(pv[0, pl.ds(pl.multiple_of(c * BLK, BLK), BLK), :])
+        vsrc[...] = pack_tri(upper_inverse(pv[0, pl.ds(pl.multiple_of(c * BLK, BLK), BLK), :]))
         usrc[...] = jnp.concatenate([pv[0, pl.ds(0, HALF), :], pv[0, pl.ds(HALF, HALF), :]], axis=1)
 
     pl.semaphore_wait(barrier, jnp.where(is_src, 14, jnp.where(is_deputy, 28, 21)))
@@ -174,19 +187,19 @@
         return remote(group, gathered.at[z], sb.at[k], rb.at[z], in_line(k))
 
     def send_vy(k):
-        return remote(vsrc.at[my_rows], gv.at[c, my_rows], svy.at[k], rv1, at(0, k, c, x))
+        return remote(vsrc.at[tri_rows], gv.at[c, tri_rows], svy.at[k], rv1, at(0, k, c, x))
 
     def send_uy(k):
         return remote(usrc.at[my_rows], gu.at[my_rows], suy.at[k], ru1, at(0, k, c, x))
 
     def send_vz(k):
-        return remote(gv.at[c, my_rows], gv.at[c, my_rows], svz.at[k], rv1, at(k, y, c, x))
+        return remote(gv.at[c, tri_rows], gv.at[c, tri_rows], svz.at[k], rv1, at(k, y, c, x))
 
     def send_uz(k):
         return remote(gu.at[my_rows], gu.at[my_rows], suz.at[k], ru1, at(k, y, c, x))
 
     def send_vx(k):
-        return remote(gv.at[c, my_rows], gv.at[c, my_rows], svx.at[k], rvx.at[c, x], in_cross(k))
+        return remote(gv.at[c, tri_rows], gv.at[c, tri_rows], svx.at[k], rvx.at[c, x], in_cross(k))
 
     def send_ux(k):
         return remote(gu.at[my_rows], gu.at[my_rows], sux.at[k], rux.at[x], in_cross(k))
@@ -201,7 +214,7 @@
     @pl.when(is_src)
     def _():
         start(send_vy, NY)
-        gv[c, my_rows, :] = vsrc[my_rows, :]
+        gv[c, tri_rows, :] = vsrc[tri_rows, :]
 
     @pl.when(is_src & (c == 1))
     def _():
@@ -279,7 +292,7 @@
 
     def wait_v(cc):
         for k in range(NX):
-            rows = pl.ds(k * PIECE, PIECE)
+            rows = pl.ds(k * TRI_PIECE, TRI_PIECE)
 
             @pl.when(jnp.logical_or(x != k, c != cc))
             def _():
@@ -445,9 +458,9 @@
             pltpu.VMEM((3 * BLK, COLS), BF16),
             pltpu.VMEM((3 * BLK, COLS), BF16),
             pltpu.VMEM((BLK, COLS), F32),
-            pltpu.VMEM((HALF, TRI), F32),
+            pltpu.VMEM((STRIP, TRI), F32),
             pltpu.VMEM((HALF, SQ), F32),
-            pltpu.VMEM((2, HALF, TRI), F32),
+            pltpu.VMEM((2, STRIP, TRI), F32),
             pltpu.VMEM((HALF, SQ), F32),
             dma((6,)),
             dma((8,)), dma((8,)), dma((8,)), dma((8,)),

time: 29.7 us -> 29.4 us (0.990); the launches traced: 29.6 us -> 28.9 us
  Pallas kernels: 29.4 us -> 28.8 us
    pallas_call x1, Pallas kernels: 24.6 us -> 24 us  [per_device(): pl.pallas_call(gather_kernel, out_shape=(pltpu.VMEM((TESTS, COLS), F32),...]
where the time goes in v5:
time: 29.4 us; the launch traced here: 28.9 us
  Pallas kernels  28.8 us (98%)
    pallas_call x1, Pallas kernels, per_device(): pl.pallas_call(gather_kernel, out_shape=(pltpu.VMEM((TESTS, COLS), F32),...  24 us
    pallas_call x1, Pallas kernels, per_device(): pl.pallas_call(finish_kernel, out_shape=jax.ShapeDtypeStruct((ROUNDS, TES...  4.78 us

profile of v5, /device:TPU:37, one launch (start us, length us, event | category | flops | bytes accessed | tf_op | source)
XLA Modules:
  0.0 28.9 jit_solution(14177213627785805783)
XLA Ops:
  0.0 24.0 %gather_and_half.1 = (f32[2048,1024]{1,0:T(8,128)S(1)}, bf16[2048,768]{1,0:T(8,128)(2,1)S(1)}, bf16[768,1024]{1,0:T(8,128)(2,1)S(1)}) custom-call(f32[8,4,16384]{2,1,0:T(4,128)} %train.1, f32[8]{0:T(128)} %scales_hbm.1, f32[8,1,32]{2,1,0:T(1,128)} %tests_hbm.1, f32[4,512,256]{2,1,0:T(8,128)} %panel.1), custom_call_target="tpu_custom_call" | custom-call | tf_op jit(solution)/shard_map/gather_and_half/pallas_call | solution.py:434
  24.0 4.8 %finish.1 = f32[4,2048,256]{2,1,0:T(8,128)} custom-call(f32[2048,1024]{1,0:T(8,128)S(1)} %get-tuple-element.8.acc, bf16[2048,768]{1,0:T(8,128)(2,1)S(1)} %get-tuple-element.9.a0, bf16[768,1024]{1,0:T(8,128)(2,1)S(1)} %get-tuple-element.10.w0), custom_call_target="tpu_custom_call" | custom-call | tf_op jit(solution)/shard_map/finish/pallas_call | solution.py:476
